TPU v7x, 32 devices: a whole 2x2x4 slice. The times are simulated.
32 devices in a mesh: dp: 4 (over y, core), cent: 8 (over z, x).
Axes of the slice: x: 2, y: 2, z: 4, core: 2. Of those that a mesh axis runs over, the one named last changes fastest.
Arguments:
- fragments: bfloat16 [8192, 1024], P(('dp', 'cent')), may hold values from -1500 to 1500
- order: int32 [32, 256], P(('dp', 'cent')), may hold values from 0 to 255, each once within a row
- group_ids: int32 [8192, 1], P(('dp', 'cent')), may hold values from 0 to 7; in each aligned block of 256 rows (0 to 255, 256 to 511, ...) at most 64 rows name the same one
- w_first: bfloat16 [1024, 1024], replicated, may hold values from -0.1875 to 0.1875
- w_second: bfloat16 [1024, 256], replicated, may hold values from -0.1875 to 0.1875
- centroids: float32 [8192, 256], P('cent'), may hold values from -24 to 24
Outputs:
- centroids_out: float32 [8192, 256], P('cent')
Inputs may be any that keep to these rules, and one draw needn't show every extreme that they name: `order`: each row is a permutation of 0 to 255. `group_ids`: among the rows of one device (aligned blocks of 256 rows) no group is named by more than 64 rows, a bound that some block reaches.
All inputs are finite; a program needn't handle non-finite values.
Results may differ from a plain program's by a relative error of at most 0.0075.
Values may be sent and summed in bfloat16 or wider, within the bound.
A program may use at most 64 MiB of HBM per device.

v0:
```python
import jax
import jax.numpy as jnp
from jax import lax
from jax.sharding import PartitionSpec as P

STEPS = 2
beta_scale = 0.0625
prior_weight = 1.0
eps_value = 1e-05


def per_device(fragments, order, group_ids, w_first, w_second, centroids):
    rows_here = fragments.shape[0]
    picked = jnp.take(fragments, order[0], axis=0)
    hidden = jax.nn.gelu(
        jnp.dot(picked, w_first, preferred_element_type=jnp.float32), approximate=True
    ).astype(jnp.bfloat16)
    proj = jnp.dot(hidden, w_second, preferred_element_type=jnp.float32)
    total_rows = float(rows_here * lax.axis_size("dp") * lax.axis_size("cent"))
    mean = lax.psum(jnp.sum(proj, axis=0), ("dp", "cent")) / total_rows
    var = lax.psum(jnp.sum((proj - mean) ** 2, axis=0), ("dp", "cent")) / total_rows
    zrows = ((proj - mean) * lax.rsqrt(var + eps_value)).astype(jnp.bfloat16)
    width = zrows.shape[1]
    groups = group_ids[:, 0]
    group_count = lax.axis_size("cent")
    capacity = 2 * rows_here // group_count
    member = (groups[:, None] == jnp.arange(group_count, dtype=jnp.int32)[None, :]).astype(
        jnp.float32
    )
    index = jnp.arange(rows_here, dtype=jnp.int32)
    before = (index[:, None] > index[None, :]).astype(jnp.float32)
    rank = jnp.sum(jnp.dot(before, member) * member, axis=1).astype(jnp.int32)
    slot = groups * capacity + rank
    place = (slot[:, None] == jnp.arange(group_count * capacity, dtype=jnp.int32)[None, :]).astype(
        jnp.bfloat16
    )
    packed = lax.dot_general(
        place, zrows, (((0,), (0,)), ((), ())), preferred_element_type=jnp.float32
    ).astype(jnp.bfloat16)
    filled = jnp.sum(place.astype(jnp.float32), axis=0).astype(jnp.bfloat16)
    received, live = (
        lax.all_to_all(
            packed.reshape(group_count, capacity, width),
            "cent",
            split_axis=0,
            concat_axis=0,
            tiled=True,
        ),
        lax.all_to_all(
            filled.reshape(group_count, capacity), "cent", split_axis=0, concat_axis=0, tiled=True
        ),
    )
    received = received.reshape(group_count * capacity, width)
    live_rows = live.reshape(group_count * capacity).astype(jnp.float32)
    current = centroids
    parts_dp = lax.axis_size("dp")
    where_dp = lax.axis_index("dp")
    for step in range(STEPS):
        rounded = current.astype(jnp.bfloat16)
        cnorm = jnp.sum(current * current, axis=1)
        cross = lax.dot_general(
            received, rounded, (((1,), (1,)), ((), ())), preferred_element_type=jnp.float32
        )
        scores = beta_scale * (2.0 * cross - cnorm[None, :])
        top = jnp.max(scores, axis=1, keepdims=True)
        expo = jnp.exp(scores - top)
        resp = (expo / jnp.sum(expo, axis=1, keepdims=True) * live_rows[:, None]).astype(
            jnp.bfloat16
        )
        num = lax.dot_general(
            resp, received, (((0,), (0,)), ((), ())), preferred_element_type=jnp.float32
        )
        den = jnp.sum(resp.astype(jnp.float32), axis=0)
        share = current.shape[0] // parts_dp
        num_part, den_part = (
            lax.psum_scatter(num, "dp", scatter_dimension=0, tiled=True),
            lax.psum_scatter(den, "dp", scatter_dimension=0, tiled=True),
        )
        old = lax.dynamic_slice_in_dim(current, where_dp * share, share, 0)
        fresh = (num_part + prior_weight * old) / (den_part + prior_weight)[:, None]
        current = lax.all_gather(fresh, "dp", axis=0, tiled=True)
    return current


def solution(mesh):
    return jax.shard_map(
        per_device,
        mesh=mesh,
        in_specs=(
            P(("dp", "cent"), None),
            P(("dp", "cent"), None),
            P(("dp", "cent"), None),
            P(),
            P(),
            P("cent", None),
        ),
        out_specs=P("cent", None),
        check_vma=False,
    )
```

profile of v0, /device:TPU:0, one launch (start us, length us, event | category | flops | bytes accessed | tf_op | source)
XLA Modules:
  0.0 222.9 jit_solution(5794457838258072373)
XLA Ops:
  6.5 1.0 fusion.2
  7.6 0.7 multiply_add_fusion
  9.1 7.3 %all-to-all-start.1 = ((bf16[8,1,64]{2,1,0:T(2,128)(2,1)}), bf16[8,1,64]{2,1,0:T(2,128)(2,1)S(1)}, u32[]{:S(2)}, u32[]{:S(2)}) async-start(bf16[8,1,64]{2,1,0:T(2,128)(2,1)} %all_to_all.12), calls=%async_computation.1 | async-start | bytes 8192 | tf_op jit(solution)/shard_map/all_to_all | solution.py:49
  17.0 0.7 compare_and_fusion
  17.7 3.5 %gather_fusion = bf16[256,1024]{1,0:T(8,128)(2,1)} fusion(bf16[256,1024]{1,0:T(8,128)(2,1)} %param.6, s32[1024]{0:T(1024)S(1)} %pad_clamp_fusion), kind=kCustom, calls=%fused_computation | custom fusion | bytes 1049600 | tf_op jit(solution)/shard_map/jit(_take)/gather | solution.py:14
  21.2 2.4 %fusion.36 = (f32[256]{0:T(256)S(1)}, f32[256,256]{1,0:T(8,128)S(1)}) fusion(bf16[1024,256]{1,0:T(8,128)(2,1)} %param.10, bf16[1024,1024]{1,0:T(8,128)(2,1)S(1)} %copy-done, bf16[256,1024]{1,0:T(8,128)(2,1)} %gather_fusion, pred[256]{0:T(512)(128)(4,1)S(1)} %compare_and_fusion), kind=kOutput, calls=%fused_computation.60 | convolution fusion | flops 673775360 | bytes 3409152 | tf_op jit(solution)/shard_map/dot_general | solution.py:18
  23.6 40.8 %psum.14 = f32[256]{0:T(256)S(1)} all-reduce(f32[256]{0:T(256)S(1)} %get-tuple-element.9), channel_id=1, replica_groups=mesh['dp'=4,'cent'=8] {'dp','cent'}, use_global_device_ids=true, to_apply=%region_2.3 | all-reduce | flops 256 | bytes 2048 | tf_op jit(solution)/shard_map/psum | solution.py:20
  64.5 40.0 %psum.15 = f32[256]{0:T(256)S(1)} all-reduce(f32[256]{0:T(256)S(1)} %multiply_reduce_fusion.2), channel_id=1, replica_groups=mesh['dp'=4,'cent'=8] {'dp','cent'}, use_global_device_ids=true, to_apply=%region_4.5 | all-reduce | flops 256 | bytes 2048 | tf_op jit(solution)/shard_map/psum | solution.py:21
  104.6 1.1 convolution_convert_fusion
  105.7 5.3 %all-to-all-start = ((bf16[8,64,256]{2,1,0:T(8,128)(2,1)}), bf16[8,64,256]{2,1,0:T(8,128)(2,1)S(1)}, u32[]{:S(2)}, u32[]{:S(2)}) async-start(bf16[8,64,256]{2,1,0:T(8,128)(2,1)} %bitcast.22), calls=%async_computation | async-start | bytes 524288 | tf_op jit(solution)/shard_map/all_to_all | solution.py:42
  111.4 7.9 %all-to-all-done = bf16[8,64,256]{2,1,0:T(8,128)(2,1)S(1)} async-done(((bf16[8,64,256]{2,1,0:T(8,128)(2,1)}), bf16[8,64,256]{2,1,0:T(8,128)(2,1)S(1)}, u32[]{:S(2)}, u32[]{:S(2)}) %all-to-all-start) | async-done | bytes 262176 | tf_op jit(solution)/shard_map/all_to_all | solution.py:42
  121.0 1.5 fusion.41
  123.8 5.7 %all-reduce = f32[1024]{0:T(1024)S(1)} all-reduce(f32[1024]{0:T(1024)S(1)} %get-tuple-element.7), channel_id=3, replica_groups=mesh['dp'=4,'cent'=8] {'dp'}, use_global_device_ids=true, to_apply=%region_11.12.clone | all-reduce | flops 1024 | bytes 8192
  129.6 16.2 %reduce-scatter.3.cloned.1.call-done = f32[256,256]{1,0:T(8,128)} async-done(((f32[1024,256]{1,0:T(8,128)}), f32[256,256]{1,0:T(8,128)}) %reduce-scatter.3.cloned.1.call-update) | async-done | bytes 262160 | tf_op jit(solution)/shard_map/reduce_scatter | solution.py:76
  145.8 1.8 add_divide_fusion.1
  147.6 16.8 %all-gather.3.cloned.1.call-done = f32[1024,256]{1,0:T(8,128)} async-done(((f32[256,256]{1,0:T(8,128)}), f32[1024,256]{1,0:T(8,128)}) %all-gather.3.cloned.1.call-update) | async-done | bytes 1048592 | tf_op jit(solution)/shard_map/all_gather | solution.py:81
  164.5 1.4 multiply_reduce_fusion
  165.9 1.8 fusion.40
  168.9 1.5 fusion.42
  170.4 5.9 %all-reduce.1 = f32[1024]{0:T(1024)S(1)} all-reduce(f32[1024]{0:T(1024)S(1)} %get-tuple-element.5), channel_id=5, replica_groups=mesh['dp'=4,'cent'=8] {'dp'}, use_global_device_ids=true, to_apply=%region_17.18.clone | all-reduce | flops 1024 | bytes 8192
  176.4 19.0 %reduce-scatter.5.cloned.1.call-done = f32[256,256]{1,0:T(8,128)} async-done(((f32[1024,256]{1,0:T(8,128)}), f32[256,256]{1,0:T(8,128)}) %reduce-scatter.5.cloned.1.call-update) | async-done | bytes 262160 | tf_op jit(solution)/shard_map/reduce_scatter | solution.py:76
  195.4 1.8 add_divide_fusion
  197.3 16.9 %all-gather.5.cloned.1.call-done = f32[1024,256]{1,0:T(8,128)} async-done(((f32[256,256]{1,0:T(8,128)}), f32[1024,256]{1,0:T(8,128)}) %all-gather.5.cloned.1.call-update) | async-done | bytes 1048592 | tf_op jit(solution)/shard_map/all_gather | solution.py:81
  214.1 2.3 %copy.10 = f32[1024,256]{1,0:T(8,128)} copy(f32[1024,256]{1,0:T(8,128)} %all-gather.5.cloned.1.call-done) | data formatting | bytes 2097152
  (34 shorter events, 5.8 us)
Async XLA Ops:
  6.5 14.7 %copy-start = (bf16[1024,1024]{1,0:T(8,128)(2,1)S(1)}, bf16[1024,1024]{1,0:T(8,128)(2,1)}, u32[]{:S(2)}) copy-start(bf16[1024,1024]{1,0:T(8,128)(2,1)} %param.9) | copy-start | bytes 6291460
  9.1 96.6 %all-to-all-start.1 = ((bf16[8,1,64]{2,1,0:T(2,128)(2,1)}), bf16[8,1,64]{2,1,0:T(2,128)(2,1)S(1)}, u32[]{:S(2)}, u32[]{:S(2)}) async-start(bf16[8,1,64]{2,1,0:T(2,128)(2,1)} %all_to_all.12), calls=%async_computation.1 | async-start | bytes 8192 | tf_op jit(solution)/shard_map/all_to_all | solution.py:49
  21.2 89.9 %copy-start.1 = (f32[1024,256]{1,0:T(8,128)S(1)}, f32[1024,256]{1,0:T(8,128)}, u32[]{:S(2)}) copy-start(f32[1024,256]{1,0:T(8,128)} %param.11) | copy-start | bytes 3145732
  105.7 13.6 %all-to-all-start = ((bf16[8,64,256]{2,1,0:T(8,128)(2,1)}), bf16[8,64,256]{2,1,0:T(8,128)(2,1)S(1)}, u32[]{:S(2)}, u32[]{:S(2)}) async-start(bf16[8,64,256]{2,1,0:T(8,128)(2,1)} %bitcast.22), calls=%async_computation | async-start | bytes 524288 | tf_op jit(solution)/shard_map/all_to_all | solution.py:42
  111.0 34.8 %reduce-scatter.3.cloned.1.call-start = ((), (), s32[]{:S(2)}) async-start(), calls=%async_computation.4 | async-start | bytes 1310720 | tf_op jit(solution)/shard_map/reduce_scatter | solution.py:76
  121.0 1.5 copy-start.2
  122.5 42.0 %all-gather.3.cloned.1.call-start = ((), (), s32[]{:S(2)}) async-start(), calls=%async_computation.5 | async-start | bytes 1310720 | tf_op jit(solution)/shard_map/all_gather | solution.py:81
  147.6 47.8 %reduce-scatter.5.cloned.1.call-start = ((), (), s32[]{:S(2)}) async-start(), calls=%async_computation.6 | async-start | bytes 1310720 | tf_op jit(solution)/shard_map/reduce_scatter | solution.py:76
  170.3 43.8 %all-gather.5.cloned.1.call-start = ((), (), s32[]{:S(2)}) async-start(), calls=%async_computation.7 | async-start | bytes 1310720 | tf_op jit(solution)/shard_map/all_gather | solution.py:81
Sparse Core Ops, SparseCore 0:
  122.6 23.1 reduce-scatter.2
  147.7 16.7 all-gather.2
  170.5 24.8 reduce-scatter.4
  197.4 16.7 all-gather.4
where the time goes:
time: 224 us; the launch traced here: 223 us
  blocking collectives  92.4 us (41%)
  waiting for transfers between devices  77 us (34%)
  between operations  13.9 us (6%)
  starting transfers between devices  12.7 us (6%)
  other arithmetic  9.96 us (4%)
  matrix products  9.85 us (4%)
  local copies, waits for them, and re-layouts  7.14 us (3%)
    psum x1, blocking collectives, per_device(): mean = lax.psum(jnp.sum(proj, axis=0), ('dp', 'cent')) / total_rows  40.8 us
    psum x1, blocking collectives, per_device(): lax.psum(jnp.sum((proj - mean) ** 2, axis=0), ('dp', 'cent')) / total_rows  40 us
    reduce_scatter x2, waiting for transfers between devices, per_device(): lax.psum_scatter(num, 'dp', scatter_dimension=0, tiled=True)  35.3 us
    all_gather x2, waiting for transfers between devices, per_device(): current = lax.all_gather(fresh, 'dp', axis=0, tiled=True)  33.7 us
    unnamed x2, blocking collectives  11.6 us
    all_to_all x1, waiting for transfers between devices, per_device(): lax.all_to_all(packed.reshape(group_count, capacity, width), 'cent', spli...  7.92 us
    all_to_all x1, starting transfers between devices, per_device(): lax.all_to_all(filled.reshape(group_count, capacity), 'cent', split_axis=...  7.25 us
    all_to_all x1, starting transfers between devices, per_device(): lax.all_to_all(packed.reshape(group_count, capacity, width), 'cent', spli...  5.31 us
  transfers between devices with their start and end apart: 6, of which 5 were waited for; matrix products, arithmetic and copies ran while one was open for 4% of the time, Pallas kernels for 0%

commit v1 on v0

--- a/solution.py
+++ b/solution.py
@@ -7,6 +7,25 @@
 beta_scale = 0.0625
 prior_weight = 1.0
 eps_value = 1e-05
+
+
+def collect(x, axis, dim):
+    size, mine, width = (lax.axis_size(axis), lax.axis_index(axis), x.shape[dim])
+    right = [(i, (i + 1) % size) for i in range(size)]
+    downward = [(i, (i - 1) % size) for i in range(size)]
+    out = jnp.zeros((*x.shape[:dim], size * width, *x.shape[dim + 1 :]), x.dtype)
+    out = lax.dynamic_update_slice_in_dim(out, x, mine * width, axis=dim)
+    from_left = from_right = x
+    halfway = size // 2
+    for lap in range(1, halfway + 1):
+        from_left = lax.ppermute(from_left, axis, right)
+        out = lax.dynamic_update_slice_in_dim(out, from_left, (mine - lap) % size * width, axis=dim)
+        if lap < size - halfway:
+            from_right = lax.ppermute(from_right, axis, downward)
+            out = lax.dynamic_update_slice_in_dim(
+                out, from_right, (mine + lap) % size * width, axis=dim
+            )
+    return out
 
 
 def per_device(fragments, order, group_ids, w_first, w_second, centroids):
@@ -78,7 +97,7 @@
         )
         old = lax.dynamic_slice_in_dim(current, where_dp * share, share, 0)
         fresh = (num_part + prior_weight * old) / (den_part + prior_weight)[:, None]
-        current = lax.all_gather(fresh, "dp", axis=0, tiled=True)
+        current = collect(fresh, "dp", 0)
     return current
 
 

time: 224 us -> 215 us (0.960)
  waiting for transfers between devices: 77 us -> 65.9 us
  starting transfers between devices: 12.7 us -> 16.2 us
    all_gather x2 -> x0, waiting for transfers between devices: 33.7 us -> none  [per_device(): current = lax.all_gather(fresh, 'dp', axis=0, tiled=True)]
    ppermute x0 -> x6, waiting for transfers between devices: none -> 22.8 us  [the longest x4 22.8 us: collect(): from_left = lax.ppermute(from_left, axis, right)]
    dynamic_update_slice x0 -> x6, local copies, waits for them, and re-layouts: none -> 3.68 us  [the longest x4 2.68 us: collect(): lax.dynamic_update_slice_in_dim(out, from_left, (mine - lap) % size * wid...]
    div x2 -> x0, other arithmetic: 3.6 us -> none  [per_device(): fresh = (num_part + prior_weight * old) / (den_part + prior_weight)[:, None]]
    ppermute x0 -> x6, starting transfers between devices: none -> 3.54 us  [the longest x2 3.48 us: collect(): from_right = lax.ppermute(from_right, axis, downward)]
    dynamic_update_slice x0 -> x2, other arithmetic: none -> 2.91 us  [collect(): out = lax.dynamic_update_slice_in_dim(out, x, mine * width, axis=dim)]
    unnamed x8 -> x9, local copies, waits for them, and re-layouts: 2.92 us -> 0.67 us
  transfers between devices with their start and end apart: 6 -> 10, of which waited for: 5 -> 7; matrix products, arithmetic and copies ran while one was open for 4% -> 5% of each run, Pallas kernels for 0% -> 0%
where the time goes in v1:
time: 215 us; the launch traced here: 214 us
  blocking collectives  92.3 us (43%)
  waiting for transfers between devices  65.9 us (31%)
  starting transfers between devices  16.2 us (8%)
  between operations  14.2 us (7%)
  local copies, waits for them, and re-layouts  8.7 us (4%)
  matrix products  8.63 us (4%)
  other arithmetic  8.27 us (4%)
    psum x1, blocking collectives, per_device(): mean = lax.psum(jnp.sum(proj, axis=0), ('dp', 'cent')) / total_rows  40.8 us
    psum x1, blocking collectives, per_device(): lax.psum(jnp.sum((proj - mean) ** 2, axis=0), ('dp', 'cent')) / total_rows  40.1 us
    reduce_scatter x2, waiting for transfers between devices, per_device(): lax.psum_scatter(num, 'dp', scatter_dimension=0, tiled=True)  35.1 us
    ppermute x4, waiting for transfers between devices, collect(): from_left = lax.ppermute(from_left, axis, right)  22.8 us
    unnamed x2, blocking collectives  11.4 us
    all_to_all x1, waiting for transfers between devices, per_device(): lax.all_to_all(packed.reshape(group_count, capacity, width), 'cent', spli...  7.94 us
    all_to_all x1, starting transfers between devices, per_device(): lax.all_to_all(filled.reshape(group_count, capacity), 'cent', split_axis=...  7.25 us
    all_to_all x1, starting transfers between devices, per_device(): lax.all_to_all(packed.reshape(group_count, capacity, width), 'cent', spli...  5.31 us
  transfers between devices with their start and end apart: 10, of which 7 were waited for; matrix products, arithmetic and copies ran while one was open for 5% of the time, Pallas kernels for 0%

profile of v1, /device:TPU:0, one launch (start us, length us, event | category | flops | bytes accessed | tf_op | source)
XLA Modules:
  0.0 214.2 jit_solution(12631644457723875089)
XLA Ops:
  6.5 1.0 fusion.3
  9.1 7.3 %all-to-all-start.1 = ((bf16[8,1,64]{2,1,0:T(2,128)(2,1)}), bf16[8,1,64]{2,1,0:T(2,128)(2,1)S(1)}, u32[]{:S(2)}, u32[]{:S(2)}) async-start(bf16[8,1,64]{2,1,0:T(2,128)(2,1)} %all_to_all.12), calls=%async_computation.1 | async-start | bytes 8192 | tf_op jit(solution)/shard_map/all_to_all | solution.py:68
  17.7 3.5 %gather_fusion = bf16[256,1024]{1,0:T(8,128)(2,1)} fusion(bf16[256,1024]{1,0:T(8,128)(2,1)} %param.6, s32[1024]{0:T(1024)S(1)} %pad_clamp_fusion), kind=kCustom, calls=%fused_computation | custom fusion | bytes 1049600 | tf_op jit(solution)/shard_map/jit(_take)/gather | solution.py:33
  21.2 2.4 %fusion.38 = (f32[256]{0:T(256)S(1)}, f32[256,256]{1,0:T(8,128)S(1)}) fusion(bf16[1024,256]{1,0:T(8,128)(2,1)} %param.10, bf16[1024,1024]{1,0:T(8,128)(2,1)S(1)} %copy-done, bf16[256,1024]{1,0:T(8,128)(2,1)} %gather_fusion, pred[256]{0:T(512)(128)(4,1)S(1)} %compare_and_fusion), kind=kOutput, calls=%fused_computation.70 | convolution fusion | flops 673775360 | bytes 3409152 | tf_op jit(solution)/shard_map/dot_general | solution.py:37
  23.6 40.8 %psum.14 = f32[256]{0:T(256)S(1)} all-reduce(f32[256]{0:T(256)S(1)} %get-tuple-element.13), channel_id=1, replica_groups=mesh['dp'=4,'cent'=8] {'dp','cent'}, use_global_device_ids=true, to_apply=%region_2.3 | all-reduce | flops 256 | bytes 2048 | tf_op jit(solution)/shard_map/psum | solution.py:39
  64.5 40.1 %psum.15 = f32[256]{0:T(256)S(1)} all-reduce(f32[256]{0:T(256)S(1)} %multiply_reduce_fusion.2), channel_id=1, replica_groups=mesh['dp'=4,'cent'=8] {'dp','cent'}, use_global_device_ids=true, to_apply=%region_4.5 | all-reduce | flops 256 | bytes 2048 | tf_op jit(solution)/shard_map/psum | solution.py:40
  104.6 1.1 convolution_convert_fusion
  105.7 5.3 %all-to-all-start = ((bf16[8,64,256]{2,1,0:T(8,128)(2,1)}), bf16[8,64,256]{2,1,0:T(8,128)(2,1)S(1)}, u32[]{:S(2)}, u32[]{:S(2)}) async-start(bf16[8,64,256]{2,1,0:T(8,128)(2,1)} %bitcast.22), calls=%async_computation | async-start | bytes 524288 | tf_op jit(solution)/shard_map/all_to_all | solution.py:61
  111.4 7.9 %all-to-all-done = bf16[8,64,256]{2,1,0:T(8,128)(2,1)S(1)} async-done(((bf16[8,64,256]{2,1,0:T(8,128)(2,1)}), bf16[8,64,256]{2,1,0:T(8,128)(2,1)S(1)}, u32[]{:S(2)}, u32[]{:S(2)}) %all-to-all-start) | async-done | bytes 262176 | tf_op jit(solution)/shard_map/all_to_all | solution.py:61
  121.0 1.5 fusion.42
  123.9 5.7 %all-reduce = f32[1024]{0:T(1024)S(1)} all-reduce(f32[1024]{0:T(1024)S(1)} %get-tuple-element.11), channel_id=3, replica_groups=mesh['dp'=4,'cent'=8] {'dp'}, use_global_device_ids=true, to_apply=%region_11.12.clone | all-reduce | flops 1024 | bytes 8192
  129.6 16.2 %reduce-scatter.3.cloned.1.call-done = f32[256,256]{1,0:T(8,128)} async-done(((f32[1024,256]{1,0:T(8,128)}), f32[256,256]{1,0:T(8,128)}) %reduce-scatter.3.cloned.1.call-update) | async-done | bytes 262160 | tf_op jit(solution)/shard_map/reduce_scatter | solution.py:95
  145.9 1.8 constant_dynamic-update-slice_fusion.7
  147.7 1.7 collective-permute-start.1
  149.5 6.6 %collective-permute-done = f32[256,256]{1,0:T(8,128)} collective-permute-done((f32[256,256]{1,0:T(8,128)}, f32[256,256]{1,0:T(8,128)}, u32[]{:S(2)}, u32[]{:S(2)}) %collective-permute-start) | collective-permute-done | bytes 262176 | tf_op jit(solution)/shard_map/ppermute | solution.py:21
  157.1 1.0 constant_dynamic-update-slice_fusion.5
  158.0 4.2 %collective-permute-done.2 = f32[256,256]{1,0:T(8,128)} collective-permute-done((f32[256,256]{1,0:T(8,128)}, f32[256,256]{1,0:T(8,128)}, u32[]{:S(2)}, u32[]{:S(2)}) %collective-permute-start.2) | collective-permute-done | bytes 262176 | tf_op jit(solution)/shard_map/ppermute | solution.py:21
  165.3 1.5 fusion.43
  166.8 5.8 %all-reduce.1 = f32[1024]{0:T(1024)S(1)} all-reduce(f32[1024]{0:T(1024)S(1)} %get-tuple-element.7), channel_id=5, replica_groups=mesh['dp'=4,'cent'=8] {'dp'}, use_global_device_ids=true, to_apply=%region_17.18.clone | all-reduce | flops 1024 | bytes 8192
  172.6 18.9 %reduce-scatter.5.cloned.1.call-done = f32[256,256]{1,0:T(8,128)} async-done(((f32[1024,256]{1,0:T(8,128)}), f32[256,256]{1,0:T(8,128)}) %reduce-scatter.5.cloned.1.call-update) | async-done | bytes 262160 | tf_op jit(solution)/shard_map/reduce_scatter | solution.py:95
  191.6 1.1 constant_dynamic-update-slice_fusion.3
  192.8 1.7 collective-permute-start.4
  194.5 6.3 %collective-permute-done.3 = f32[256,256]{1,0:T(8,128)S(1)} collective-permute-done((f32[256,256]{1,0:T(8,128)S(1)}, f32[256,256]{1,0:T(8,128)S(1)}, u32[]{:S(2)}, u32[]{:S(2)}) %collective-permute-start.3) | collective-permute-done | bytes 262176 | tf_op jit(solution)/shard_map/ppermute | solution.py:21
  200.9 5.7 %collective-permute-done.5 = f32[256,256]{1,0:T(8,128)S(1)} collective-permute-done((f32[256,256]{1,0:T(8,128)S(1)}, f32[256,256]{1,0:T(8,128)S(1)}, u32[]{:S(2)}, u32[]{:S(2)}) %collective-permute-start.5) | collective-permute-done | bytes 262176 | tf_op jit(solution)/shard_map/ppermute | solution.py:21
  (49 shorter events, 10.9 us)
Async XLA Ops:
  6.5 14.6 %copy-start = (bf16[1024,1024]{1,0:T(8,128)(2,1)S(1)}, bf16[1024,1024]{1,0:T(8,128)(2,1)}, u32[]{:S(2)}) copy-start(bf16[1024,1024]{1,0:T(8,128)(2,1)} %param.9) | copy-start | bytes 6291460
  9.1 96.6 %all-to-all-start.1 = ((bf16[8,1,64]{2,1,0:T(2,128)(2,1)}), bf16[8,1,64]{2,1,0:T(2,128)(2,1)S(1)}, u32[]{:S(2)}, u32[]{:S(2)}) async-start(bf16[8,1,64]{2,1,0:T(2,128)(2,1)} %all_to_all.12), calls=%async_computation.1 | async-start | bytes 8192 | tf_op jit(solution)/shard_map/all_to_all | solution.py:68
  21.2 89.9 %copy-start.1 = (f32[1024,256]{1,0:T(8,128)S(1)}, f32[1024,256]{1,0:T(8,128)}, u32[]{:S(2)}) copy-start(f32[1024,256]{1,0:T(8,128)} %param.11) | copy-start | bytes 3145732
  105.7 13.6 %all-to-all-start = ((bf16[8,64,256]{2,1,0:T(8,128)(2,1)}), bf16[8,64,256]{2,1,0:T(8,128)(2,1)S(1)}, u32[]{:S(2)}, u32[]{:S(2)}) async-start(bf16[8,64,256]{2,1,0:T(8,128)(2,1)} %bitcast.22), calls=%async_computation | async-start | bytes 524288 | tf_op jit(solution)/shard_map/all_to_all | solution.py:61
  111.0 34.8 %reduce-scatter.3.cloned.1.call-start = ((), (), s32[]{:S(2)}) async-start(), calls=%async_computation.4 | async-start | bytes 1310720 | tf_op jit(solution)/shard_map/reduce_scatter | solution.py:95
  121.0 1.5 copy-start.3
  122.5 69.0 %reduce-scatter.5.cloned.1.call-start = ((), (), s32[]{:S(2)}) async-start(), calls=%async_computation.5 | async-start | bytes 1310720 | tf_op jit(solution)/shard_map/reduce_scatter | solution.py:95
  147.7 8.3 %collective-permute-start = (f32[256,256]{1,0:T(8,128)}, f32[256,256]{1,0:T(8,128)}, u32[]{:S(2)}, u32[]{:S(2)}) collective-permute-start(f32[256,256]{1,0:T(8,128)} %get-tuple-element.10), channel_id=1, source_target_pairs={{0,8},{8,16},{16,24},{24,0},{1,9},{9,17},{17,25},{25,1},{2,10},{10... | collective-permute-start | bytes 786440 | tf_op jit(solution)/shard_map/ppermute | solution.py:21
  147.7 9.3 %collective-permute-start.1 = (f32[256,256]{1,0:T(8,128)}, f32[256,256]{1,0:T(8,128)}, u32[]{:S(2)}, u32[]{:S(2)}) collective-permute-start(f32[256,256]{1,0:T(8,128)} %get-tuple-element.10), channel_id=1, source_target_pairs={{0,24},{8,0},{16,8},{24,16},{1,25},{9,1},{17,9},{25,17},{2,26},{10... | collective-permute-start | bytes 786440 | tf_op jit(solution)/shard_map/ppermute | solution.py:24
  156.1 6.1 %collective-permute-start.2 = (f32[256,256]{1,0:T(8,128)}, f32[256,256]{1,0:T(8,128)}, u32[]{:S(2)}, u32[]{:S(2)}) collective-permute-start(f32[256,256]{1,0:T(8,128)} %collective-permute-done), channel_id=1, source_target_pairs={{0,8},{8,16},{16,24},{24,0},{1,9},{9,17},{17,25},{25,1},{2,10},{10... | collective-permute-start | bytes 786440 | tf_op jit(solution)/shard_map/ppermute | solution.py:21
  192.7 8.1 %collective-permute-start.3 = (f32[256,256]{1,0:T(8,128)S(1)}, f32[256,256]{1,0:T(8,128)S(1)}, u32[]{:S(2)}, u32[]{:S(2)}) collective-permute-start(f32[256,256]{1,0:T(8,128)S(1)} %get-tuple-element.6), channel_id=1, source_target_pairs={{0,8},{8,16},{16,24},{24,0},{1,9},{9,17},{17,25},{25,1},{2,10},{10... | collective-permute-start | bytes 786440 | tf_op jit(solution)/shard_map/ppermute | solution.py:21
  192.8 8.1 %collective-permute-start.4 = (f32[256,256]{1,0:T(8,128)S(1)}, f32[256,256]{1,0:T(8,128)S(1)}, u32[]{:S(2)}, u32[]{:S(2)}) collective-permute-start(f32[256,256]{1,0:T(8,128)S(1)} %get-tuple-element.6), channel_id=1, source_target_pairs={{0,24},{8,0},{16,8},{24,16},{1,25},{9,1},{17,9},{25,17},{2,26},{10... | collective-permute-start | bytes 786440 | tf_op jit(solution)/shard_map/ppermute | solution.py:24
  200.8 5.8 %collective-permute-start.5 = (f32[256,256]{1,0:T(8,128)S(1)}, f32[256,256]{1,0:T(8,128)S(1)}, u32[]{:S(2)}, u32[]{:S(2)}) collective-permute-start(f32[256,256]{1,0:T(8,128)S(1)} %collective-permute-done.3), channel_id=1, source_target_pairs={{0,8},{8,16},{16,24},{24,0},{1,9},{9,17},{17,25},{25,1},{2,10},{10... | collective-permute-start | bytes 786440 | tf_op jit(solution)/shard_map/ppermute | solution.py:21
  200.9 5.7 %copy-start.2 = (f32[1024,256]{1,0:T(8,128)}, f32[1024,256]{1,0:T(8,128)S(1)}, u32[]{:S(2)}) copy-start(f32[1024,256]{1,0:T(8,128)S(1)} %constant_dynamic-update-slice_fusion.1) | copy-start | bytes 3145732
Sparse Core Ops, SparseCore 0:
  122.6 23.1 reduce-scatter.2
  166.9 24.6 reduce-scatter.4
